TPU v7x, 32 devices: a whole 2x2x4 slice. The times are simulated.
32 devices in a mesh: dp: 8 (over y, x, core), mp: 4 (over z).
Axes of the slice: x: 2, y: 2, z: 4, core: 2. Of those that a mesh axis runs over, the one named last changes fastest.
Arguments:
- tokens: bfloat16 [32, 577, 768], P(('dp', 'mp')), may hold values from -6 to 6
- lengths: int32 [32], P('dp'), may hold values from 257 to 577, as said below
- attention_norm_gain: float32 [768], replicated, may hold values from 0.5 to 1.5
- feedforward_norm_gain: float32 [768], replicated, may hold values from 0.5 to 1.5
- w_query: bfloat16 [768, 768], P(None, 'mp'), may hold values from -0.21875 to 0.21875
- w_key: bfloat16 [768, 768], P(None, 'mp'), may hold values from -0.21875 to 0.21875
- w_value: bfloat16 [768, 768], P(None, 'mp'), may hold values from -0.21875 to 0.21875
- w_out: bfloat16 [768, 768], P('mp'), may hold values from -1.75 to 1.75
- w_gate: bfloat16 [768, 2048], P(None, 'mp'), may hold values from -0.21875 to 0.21875
- w_up: bfloat16 [768, 2048], P(None, 'mp'), may hold values from -0.21875 to 0.21875
- w_down: bfloat16 [2048, 768], P('mp'), may hold values from -0.125 to 0.125
- cotangent: bfloat16 [32, 577, 768], P(('dp', 'mp')), may hold values from -6 to 6
Outputs:
- block_out: float32 [32, 577, 768], P(('dp', 'mp'))
- input_grad: float32 [32, 577, 768], P(('dp', 'mp'))
- grad_gain_attn: float32 [768], replicated
- grad_gain_mlp: float32 [768], replicated
- grad_query: float32 [768, 768], P(None, 'mp')
- grad_key: float32 [768, 768], P(None, 'mp')
- grad_value: float32 [768, 768], P(None, 'mp')
- grad_out: float32 [768, 768], P('mp')
- grad_gate: float32 [768, 2048], P(None, 'mp')
- grad_up: float32 [768, 2048], P(None, 'mp')
- grad_down: float32 [2048, 768], P('mp')
Inputs may be any that keep to these rules, and one draw needn't show every extreme that they name: `lengths`: each item's length is 257 or 577; both occur in every draw.
All inputs are finite; a program needn't handle non-finite values.
Results may differ from a plain program's by a relative error of at most 0.015.
Values may be sent and summed in bfloat16 or wider, within the bound.
A program may use at most 128 MiB of HBM per device.

v0:
```python
import functools

import jax
import jax.numpy as jnp
import numpy as np
from jax import lax
from jax.experimental import pallas as pl
from jax.experimental.pallas import tpu as pltpu
from jax.sharding import PartitionSpec as P

HEAD = 64
EPS = 1e-05
NEG = -1e30
MESH = pl.DeviceIdType.MESH
f32, bf16 = jnp.float32, jnp.bfloat16
LOOPED = ("A", "F", "B")
SLOTS = (3, 6, 8, 12)
STEPS = ((3, 3, 3), (2, 3, 3), (2, 3, 3))

PLAN = {
    ("P", 0, 0): (("s", 0),),
    ("A", 0, 0): (("s", 1),),
    ("A", 0, 2): (("a", 1, 0, 0),),
    ("A", 1, 0): (("a", 1, 1, 0), ("a", 1, 2, 0), ("a", 1, 0, 1), ("a", 2, 0, 0), ("a", 2, 1, 0), ("a", 1, 1, 1), ("a", 1, 2, 1), ("a", 2, 0, 1), ("a", 2, 2, 0), ("a", 1, 0, 2), ("a", 1, 0, 3), ("a", 3, 0, 0),),
    ("A", 1, 1): (("a", 2, 1, 1), ("a", 3, 1, 0), ("a", 1, 1, 2), ("a", 1, 2, 2), ("a", 2, 2, 1), ("a", 2, 0, 2), ("a", 1, 1, 3), ("a", 3, 0, 1), ("a", 1, 2, 3), ("a", 3, 2, 0),),
    ("A", 1, 2): (("a", 2, 0, 3), ("s", 2),),
    ("A", 2, 0): (("a", 2, 1, 2), ("a", 3, 1, 1),),
    ("A", 2, 1): (("a", 2, 1, 3), ("a", 2, 2, 2), ("a", 3, 0, 2), ("a", 3, 2, 1), ("g", 1, 1, 0),),
    ("A", 2, 2): (("a", 2, 2, 3), ("a", 3, 0, 3),),
    ("A", 3, 0): (("a", 3, 1, 2), ("g", 1, 2, 0),),
    ("A", 3, 1): (("a", 3, 1, 3), ("a", 3, 2, 2),),
    ("A", 3, 2): (("a", 3, 2, 3), ("g", 1, 1, 1), ("g", 1, 3, 0),),
    ("F", 0, 0): (("g", 1, 1, 2), ("g", 1, 2, 1),),
    ("F", 0, 2): (("p", 0), ("g", 1, 3, 1), ("g", 2, 1, 0),),
    ("F", 0, 3): (("g", 2, 2, 0),),
    ("F", 0, 4): (("p", 1), ("t", 0, 0),),
    ("F", 1, 0): (("g", 1, 2, 2), ("t", 1, 0), ("g", 2, 3, 0), ("g", 1, 2, 3), ("g", 2, 2, 1), ("g", 1, 3, 2), ("g", 2, 3, 1), ("g", 2, 1, 1), ("g", 1, 3, 3), ("g", 2, 1, 2),),
    ("F", 1, 2): (("p", 2), ("t", 0, 1), ("t", 1, 1),),
    ("F", 1, 3): (("g", 2, 2, 2),),
    ("F", 1, 4): (("p", 3), ("g", 2, 3, 2), ("t", 2, 0),),
    ("F", 2, 0): (("g", 2, 2, 3),),
    ("F", 2, 1): (("g", 2, 3, 3), ("t", 3, 0), ("t", 0, 2), ("t", 1, 2),),
    ("F", 2, 2): (("p", 4),),
    ("F", 2, 4): (("p", 5), ("t", 2, 1), ("t", 4, 0),),
    ("F", 3, 1): (("t", 3, 1), ("t", 5, 0),),
    ("F", 3, 2): (("p", 6),),
    ("F", 3, 4): (("p", 7), ("t", 2, 2), ("t", 6, 0),),
    ("B", 0, 0): (("t", 7, 0),),
    ("B", 0, 7): (("p", 8), ("t", 3, 2), ("t", 4, 1),),
    ("B", 0, 8): (("p", 9), ("t", 5, 1), ("t", 8, 0),),
    ("B", 0, 9): (("p", 10), ("t", 6, 1), ("t", 9, 0),),
    ("B", 1, 7): (("p", 11), ("t", 4, 2), ("t", 5, 2), ("t", 7, 1), ("t", 8, 1), ("t", 10, 0), ("t", 11, 0), ("t", 9, 1), ("t", 6, 2),),
    ("B", 1, 8): (("p", 12),),
    ("B", 1, 9): (("p", 13), ("t", 8, 2), ("t", 9, 2), ("t", 12, 0), ("t", 10, 1), ("t", 11, 1), ("t", 7, 2), ("t", 13, 0),),
    ("B", 2, 7): (("p", 14),),
    ("B", 2, 8): (("p", 15), ("t", 10, 2), ("t", 11, 2), ("t", 12, 1), ("t", 13, 1), ("t", 14, 0),),
    ("B", 2, 9): (("p", 16), ("t", 15, 0),),
    ("B", 3, 7): (("p", 17), ("t", 12, 2), ("t", 13, 2), ("t", 14, 1), ("t", 15, 1), ("t", 16, 0), ("f", 1, 0), ("t", 17, 0),),
    ("B", 3, 8): (("p", 18),),
    ("B", 3, 9): (("p", 19), ("t", 14, 2), ("t", 15, 2), ("t", 18, 0),),
    ("E", 0, 0): (("t", 16, 1), ("t", 17, 1), ("t", 19, 0), ("f", 1, 1), ("f", 2, 0),),
    ("E", 0, 1): (("n", 0),),
    ("E", 0, 2): (("n", 1),),
    ("E", 0, 3): (("t", 18, 1), ("t", 16, 2),),
    ("E", 0, 4): (("t", 17, 2),),
    ("E", 0, 5): (("n", 2), ("t", 19, 1),),
    ("E", 0, 6): (("f", 3, 0),),
    ("E", 0, 7): (("t", 18, 2), ("f", 2, 1), ("f", 4, 0), ("n", 3), ("f", 1, 2), ("t", 19, 2), ("f", 5, 0), ("f", 3, 1), ("f", 1, 3), ("f", 4, 1), ("n", 4), ("f", 5, 1), ("f", 3, 2), ("f", 2, 2), ("f", 3, 3), ("f", 4, 2), ("f", 5, 2), ("f", 2, 3), ("f", 4, 3), ("f", 5, 3),),
}


def nn(left, right):
    return lax.dot_general(left, right, (((1,), (0,)), ((), ())), preferred_element_type=f32)


def nt(left, right):
    return lax.dot_general(left, right, (((1,), (1,)), ((), ())), preferred_element_type=f32)


def iota(shape, axis):
    return lax.broadcasted_iota(jnp.int32, shape, axis)


def turned(w, low):
    return jnp.where(low, -pltpu.roll(w, 96, 1), pltpu.roll(w, 32, 1))


def swap(w):
    return pltpu.roll(w, 64, 1)


def order_table(count):
    return [sorted(range(count), key=lambda s: s ^ z) for z in range(count)]


def pick(table, row, column):
    found = 0
    for r, values in enumerate(table):
        for c, value in enumerate(values):
            found = found + jnp.where((row == r) & (column == c), value, 0)
    return found


def kernel(
    mp,
    T,
    len_ref,
    x_ref,
    dy_ref,
    g1_ref,
    g2_ref,
    cos_ref,
    sin_ref,
    wq_ref,
    wk_ref,
    wv_ref,
    wo_ref,
    wg_ref,
    wu_ref,
    wd_ref,
    out_ref,
    dx_ref,
    ga_ref,
    gm_ref,
    fin_ref,
    w,
    n1,
    n2,
    n2t,
    dyb,
    q,
    k,
    v,
    kt,
    ctx,
    outs,
    heads_t,
    lse,
    mask,
    hb,
    turned_rows,
    made,
    acc,
    res,
    dn,
    dk_sum,
    dv_sum,
    gbuf,
    r1,
    r2,
    r3,
    r4,
    total,
    gain_in,
    staged,
    own_sem,
    az_send,
    az_recv,
    ag_send,
    ag_recv,
    z_send,
    z_recv,
    g_send,
    g_recv,
    s_send,
    s_recv,
    h_send,
    h_recv,
    fin_sem,
    f_send,
    f_recv,
    gain_send,
    gain_recv,
    out_sem,
    credit,
):
    seq, width = x_ref.shape[1], x_ref.shape[2]
    half, quarter, eighth = width // 2, width // 4, width // 8
    heads = wq_ref.shape[0] // HEAD
    tall = width // heads
    blocks = [(a, min(a + 256, T)) for a in range(0, T, 256)]
    dp_at, z = lax.axis_index("dp"), lax.axis_index("mp")
    core, bit1, bit2 = dp_at % 2, (dp_at // 2) % 2, (dp_at // 4) % 2
    partner = dp_at + 1 - 2 * core
    flip1, flip2 = dp_at + 2 - 4 * bit1, dp_at + 4 - 8 * bit2
    near = jnp.where(core == 0, flip1, flip2)
    far = jnp.where(core == 0, flip2, flip1)
    near_bit = jnp.where(core == 0, bit1, bit2)
    far_bit = jnp.where(core == 0, bit2, bit1)
    table = order_table(mp)
    units_f, units = 2 * mp, 3 * mp

    def at(start, size):
        return pl.ds(pl.multiple_of(start, 16), size)

    def spans(start, size):
        half_at = start + core * (size // 2)
        quarter_at = half_at + far_bit * (size // 4)
        eighth_at = quarter_at + near_bit * (size // 8)
        return (near, at(eighth_at, size // 8)), (far, at(quarter_at, size // 4)), (partner, at(half_at, size // 2))

    widening = spans(0, width)
    by_head = [spans(h * tall, tall) for h in range(heads)]
    brief = ((near, at(core * half + (bit1 + bit2) % 2 * quarter, quarter)), widening[2])
    direct = (widening[2],)

    def remote(src, dst, send, recv, dp_to, z_to):
        return pltpu.make_async_remote_copy(
            src_ref=src,
            dst_ref=dst,
            send_sem=send,
            recv_sem=recv,
            device_id={"dp": dp_to, "mp": z_to},
            device_id_type=MESH,
        )


    def hops(kind, j):
        return (None, direct, brief, widening)[STEPS[kind][j - 1]]

    def along(kind, j, shard, to):
        part = w.at[kind, shard, hops(kind, j)[0][1]]
        return remote(part, part, z_send.at[kind, j], z_recv.at[kind, j], dp_at, to)

    def across(kind, j, shard, stage):
        to, rows = hops(kind, j)[stage]
        part = w.at[kind, shard, rows]
        return remote(part, part, g_send.at[kind, j, stage], g_recv.at[kind, j, stage], to, z)

    def head_along(j, h, shard, to):
        part = w.at[0, shard, by_head[h][0][1]]
        return remote(part, part, az_send.at[j, h], az_recv.at[j, h], dp_at, to)

    def head_across(j, h, shard, stage):
        to, rows = by_head[h][stage]
        part = w.at[0, shard, rows]
        return remote(part, part, ag_send.at[j, h, stage], ag_recv.at[j, h, stage], to, z)

    def send_own(kind):
        for j in range(1, mp):
            if kind == 0:
                for h in range(heads):
                    head_along(j, h, z, pick(table, z, j)).start()
            else:
                along(kind, j, z, pick(table, z, j)).start()

    def gather_head(j, h, stage):
        shard = pick(table, z, j)
        if stage == 0:
            head_along(j, h, shard, shard).wait_recv()
        else:
            head_across(j, h, shard, stage - 1).wait_recv()
        if stage < 3:
            head_across(j, h, shard, stage).start()

    def gather(kind, j, stage):
        shard = pick(table, z, j)
        if stage == 0:
            along(kind, j, shard, shard).wait_recv()
        else:
            across(kind, j, shard, stage - 1).wait_recv()
        if stage < STEPS[kind][j - 1]:
            across(kind, j, shard, stage).start()

    def gather_drain():
        for j in range(1, mp):
            shard = pick(table, z, j)
            for h in range(heads):
                head_along(j, h, z, shard).wait_send()
                for stage in range(3):
                    head_across(j, h, shard, stage).wait_send()
            for kind in (1, 2):
                along(kind, j, z, shard).wait_send()
                for stage in range(STEPS[kind][j - 1]):
                    across(kind, j, shard, stage).wait_send()


    def unit_of(u):
        return u if u < units_f else units_f + (u - units_f) // heads

    def head_of(u):
        return (u - units_f) % heads

    def shard_of(u):
        return pick(table, z, u // 2) if u < units_f else (z + 1 + (u - units_f) // heads) % mp

    def kind_of(u):
        return 1 + u % 2 if u < units_f else 0

    stores = (gbuf, r1, r2, r3)
    hops_back = (partner, far, near)
    given = (1 - core, 1 - far_bit, 1 - near_bit)
    kept = (core, far_bit, near_bit)

    def size_of(u, stage):
        whole = width if u < units_f else tall
        h = 0 if u < units_f else head_of(u)
        return whole >> (stage + 1), h * (whole >> stage), h * (whole >> (stage + 1))

    def give(u, stage):
        size, before, after = size_of(u, stage)
        unit = unit_of(u)
        return remote(
            stores[stage].at[unit % SLOTS[stage], at(before + given[stage] * size, size)],
            stores[stage + 1].at[unit % SLOTS[stage + 1], at(after, size)],
            s_send.at[u, stage],
            s_recv.at[u, stage],
            hops_back[stage],
            z,
        )

    def start_give(u, stage):
        if unit_of(u) >= SLOTS[stage + 1] and (u < units_f or head_of(u) == 0):
            pl.semaphore_wait(credit.at[stage], 1)
        give(u, stage).start()

    def release(u, stage):
        if unit_of(u) + SLOTS[stage + 1] < units and (u < units_f or head_of(u) == heads - 1):
            pl.semaphore_signal(
                credit.at[stage], inc=1, device_id={"dp": hops_back[stage], "mp": z}, device_id_type=MESH
            )

    def take(u, stage):
        copy = give(u, stage)
        copy.wait_recv()
        copy.wait_send()
        mine, came = stores[stage], stores[stage + 1]
        unit = unit_of(u)
        here, there = unit % SLOTS[stage], unit % SLOTS[stage + 1]
        size, before, after = size_of(u, stage)
        step = size >> (2 - stage)

        def add(i, carry):
            to = at(after + i * step, step)
            sums = mine[here, at(before + kept[stage] * size + i * step, step), :].astype(f32)
            came[there, to, :] = (sums + came[there, to, :].astype(f32)).astype(bf16)
            return carry

        lax.fori_loop(0, (4, 2, 1)[stage], add, 0)
        if stage > 0:
            release(u, stage - 1)
        if stage < 2:
            start_give(u, stage + 1)
        elif own_shard(u):
            rows = pl.ds(after, size)
            r4[kind_of(u), z, rows, :] = r3[there, rows, :]
        else:
            home(u).start()

    def own_shard(u):
        return u < 2 or u >= units_f + (mp - 1) * heads

    def home(u):
        size, _, after = size_of(u, 2)
        kind, rows = kind_of(u), pl.ds(after, size)
        arrived = kind if u < units_f else 3 + head_of(u)
        return remote(
            r3.at[unit_of(u) % SLOTS[3], rows],
            r4.at[kind, z, rows],
            h_send.at[u],
            h_recv.at[arrived, z],
            dp_at,
            shard_of(u),
        )

    def home_drain():
        for u in range(units_f + mp * heads):
            if not own_shard(u):
                home(u).wait_send()


    def sum_rows(which):
        if which < 3:
            return which, pl.ds(0, eighth), widening
        return 0, pl.ds((which - 3) * (tall // 8), tall // 8), by_head[which - 3]

    def fin_own(which):
        kind, rows, spans_of = sum_rows(which)
        return pltpu.make_async_copy(total.at[kind, rows], fin_ref.at[kind, spans_of[0][1]], fin_sem.at[which])

    def fin_across(which, stage):
        kind, own_rows, spans_of = sum_rows(which)
        to, rows = spans_of[stage]
        src = total.at[kind, own_rows] if stage == 0 else fin_ref.at[kind, rows]
        return remote(src, fin_ref.at[kind, rows], f_send.at[which, stage], f_recv.at[which, stage], to, z)

    def finish(which, stage):
        kind, rows, _ = sum_rows(which)
        if stage == 0:
            for src in range(mp):

                @pl.when(z != src)
                def _(src=src):
                    remote(
                        r3.at[0, rows], r4.at[kind, src, rows], h_send.at[0], h_recv.at[which, src], dp_at, src
                    ).wait_recv()

            sums = r4[kind, 0, rows, :].astype(f32)
            for src in range(1, mp):
                sums = sums + r4[kind, src, rows, :].astype(f32)
            total[kind, rows, :] = sums.astype(bf16)
            fin_own(which).start()
        else:
            if stage == 1:
                fin_own(which).wait()
            fin_across(which, stage - 1).wait_recv()
        if stage < 3:
            fin_across(which, stage).start()

    def finish_drain(which):
        for stage in range(3):
            fin_across(which, stage).wait_send()


    def gain_copy(stage):
        to = (partner, far, near)[stage]
        return remote(gain_in.at[0], gain_in.at[1 + stage], gain_send.at[stage], gain_recv.at[stage], to, z)

    def gain_along(i):
        return remote(
            gain_in.at[0], gain_in.at[3 + i], gain_send.at[2 + i], gain_recv.at[2 + i], dp_at, (z + i) % mp
        )

    def gain_step(stage):
        if stage in (1, 2, 3):
            gain_copy(stage - 1).wait()
            gain_in[0] = gain_in[0] + gain_in[stage]
        if stage < 3:
            gain_copy(stage).start()
        elif stage == 3:
            for i in range(1, mp):
                gain_along(i).start()
        else:
            for i in range(1, mp):
                gain_along(i).wait()
            sums = gain_in[0]
            for i in range(1, mp):
                sums = sums + gain_in[3 + i]
            ga_ref[...] = sums[0]
            gm_ref[...] = sums[1]

    move = {"p": lambda u: start_give(u, 0), "s": send_own, "a": gather_head, "g": gather, "t": take, "f": finish, "n": gain_step}

    def place(part, step, i):
        def run(acts):
            for name, *what in acts:
                move[name](*what)

        if isinstance(step, int):
            run(PLAN.get((part, step, i), ()))
            return
        for at_step in range(mp):
            acts = PLAN.get((part, at_step, i))
            if acts is not None:
                pl.when(step == at_step)(functools.partial(run, acts))

    def run_steps(part, body):
        if part in LOOPED:

            def again(step, carry):
                body(step)
                return carry

            lax.fori_loop(0, mp, again, 0)
        else:
            for step in range(mp):
                body(step)


    barrier = pltpu.get_barrier_semaphore()
    for to in (partner, near, far):
        pl.semaphore_signal(barrier, inc=1, device_id={"dp": to, "mp": z}, device_id_type=MESH)
    for i in range(1, mp):
        pl.semaphore_signal(
            barrier, inc=1, device_id={"dp": dp_at, "mp": (z + i) % mp}, device_id_type=MESH
        )
    hidden = wg_ref.shape[1]
    first = width - hidden
    rest = hidden - first
    pieces = [
        (ref.at[pl.ds(HEAD * h, HEAD)], w.at[0, z, pl.ds(tall * h + HEAD * i, HEAD)])
        for h in range(heads)
        for i, ref in enumerate((wq_ref, wk_ref, wv_ref, wo_ref))
    ]
    pieces += [
        (wg_ref, w.at[1, z, :, pl.ds(0, hidden)]),
        (wu_ref.at[:, pl.ds(0, first)], w.at[1, z, :, pl.ds(hidden, first)]),
        (wd_ref, w.at[2, z, pl.ds(0, hidden)]),
    ]
    stripes = width // rest
    stripe = width // stripes
    pieces += [
        (wu_ref.at[pl.ds(j * stripe, stripe), pl.ds(first, rest)], w.at[2, z, pl.ds(hidden, stripe), pl.ds(j * rest, rest)])
        for j in range(stripes)
    ]
    own = [pltpu.make_async_copy(src, dst, own_sem.at[i]) for i, (src, dst) in enumerate(pieces)]
    for copy in own:
        copy.start()

    lane = iota((T, 128), 1)
    lower = lane < 64
    low = (lane % 64) < 32
    length = len_ref[z]
    full = seq // 16 * 16

    def padded(ref):
        tail = jnp.broadcast_to(ref[0, full:seq, :].astype(f32), (T - full, width))
        tail = jnp.where(iota((T - full, width), 0) < seq - full, tail, 0.0).astype(bf16)
        return jnp.concatenate([ref[0, 0:full, :], tail], axis=0)

    def scale_of(rows_in):
        return lax.rsqrt(jnp.mean(rows_in * rows_in, axis=-1, keepdims=True) + EPS)

    def gain(ref):
        return ref[...].reshape(1, width)

    x = padded(x_ref).astype(f32)
    n1[...] = (x * scale_of(x) * gain(g1_ref)).astype(bf16)
    for copy in own[: 4 * heads]:
        copy.wait()
    pl.semaphore_wait(barrier, 3 + mp - 1)
    place("P", 0, 0)
    for copy in own[4 * heads :]:
        copy.wait()

    acc[...] = x
    dyb[...] = jnp.where(iota((T, width), 0) < length, padded(dy_ref).astype(f32), 0.0).astype(bf16)
    key_at, query_at = iota((T, T), 0), iota((T, T), 1)
    mask[...] = jnp.where((key_at <= query_at) & (key_at < length), 0.0, NEG)
    heads_t[...] = jnp.zeros_like(heads_t)
    ctx[:, heads * HEAD :, :] = jnp.zeros((mp, 256 - heads * HEAD, T), bf16)
    outs[...] = jnp.zeros_like(outs)


    def out_rows(s):
        for h in range(heads):
            outs[HEAD * h : HEAD * h + HEAD, :] = w[0, s, tall * h + 3 * HEAD : tall * h + 4 * HEAD, :]

    def attention(step):
        s = pick(table, z, step)
        cos, sin = cos_ref[...], sin_ref[...]
        for h in range(heads):
            place("A", step, h)
            qkv = nt(n1[...], w[0, s, tall * h : tall * h + tall, :])
            qk, vo = qkv[:, 0:128], qkv[:, 128:256]
            qk = qk * cos + turned(qk, low) * sin
            qh = jnp.where(lower, qk * 0.125, 0.0).astype(bf16)
            kh = jnp.where(lower, swap(qk), 0.0).astype(bf16)
            vh = jnp.where(lower, vo, 0.0).astype(bf16)
            q[s, h], k[s, h], v[s, h] = qh, kh, vh
            kt[s, h] = kh.T[0:HEAD]
            vt = vh.T[0:HEAD]
            for a, b in blocks:
                scores = nt(kh[0:b], qh[a:b]) + mask[0:b, a:b]
                peak = jnp.max(scores, axis=0, keepdims=True)
                e = jnp.exp(scores - peak)
                norm = jnp.sum(e, axis=0, keepdims=True)
                c = nn(vt[:, 0:b], e.astype(bf16))
                ctx[s, HEAD * h : HEAD * h + HEAD, a:b] = (c * (1.0 / norm)).astype(bf16)
                lse[s, h : h + 1, a:b] = peak + jnp.log(norm)
        place("A", step, heads)
        out_rows(s)
        acc[...] += nn(ctx[s].T, outs[...])

    run_steps("A", attention)

    x1 = acc[...]
    res[...] = x1
    normed = (x1 * scale_of(x1) * gain(g2_ref)).astype(bf16)
    n2[...] = normed
    n2t[...] = normed.T
    dn[...] = jnp.zeros_like(dn)


    def feed(step):
        place("F", step, 0)
        s = pick(table, z, step)
        w1, w2 = w.at[1, s], w.at[2, s]
        u0, u1 = 2 * step, 2 * step + 1
        gu = nn(n2[...], w1[...])
        late = nn(n2[:, 0:256], w2[512:768, 0:256])
        for j in range(1, 3):
            late = late + nn(n2[:, 256 * j : 256 * j + 256], w2[512:768, 256 * j : 256 * j + 256])
        dh = nt(dyb[...], w2[0:512, :])
        for i in range(2):
            part = slice(256 * i, 256 * i + 256)
            gate = gu[:, part]
            up = gu[:, 512:768] if i == 0 else late
            dhid = dh[:, part]
            sigma = 1.0 / (1.0 + jnp.exp(-gate))
            active = gate * sigma
            hb[step, :, part] = (active * up).astype(bf16)
            made[:, part] = (dhid * up * sigma * (1.0 + gate * (1.0 - sigma))).astype(bf16)
            made[:, 512 + 256 * i : 768 + 256 * i] = (dhid * active).astype(bf16)
        place("F", step, 1)
        gbuf[u0 % SLOTS[0]] = nn(n2t[...], made[:, 0:768]).astype(bf16)
        place("F", step, 2)
        turned_rows[0:512, :] = hb[step].T
        dn[...] += nt(made[:, 0:768], w1[...])
        place("F", step, 3)
        gbuf[u1 % SLOTS[0], 0:512, :] = nn(turned_rows[0:512, :], dyb[...]).astype(bf16)
        for j in range(3):
            part = slice(256 * j, 256 * j + 256)
            gbuf[u1 % SLOTS[0], 512:768, part] = nn(n2t[part, :], made[:, 768:1024]).astype(bf16)
        place("F", step, 4)
        for j in range(3):
            part = slice(256 * j, 256 * j + 256)
            dn[:, part] += nt(made[:, 768:1024], w2[512:768, part])

    run_steps("F", feed)

    place("M", 0, 0)
    x1 = res[...]
    scale = scale_of(x1)
    hat = x1 * scale
    d2 = dn[...]
    gain_in[0] = jnp.zeros_like(gain_in[0])
    gain_in[0, 1:2, :] = jnp.sum(d2 * hat, axis=0, keepdims=True)
    e = d2 * gain(g2_ref)
    dx1 = dyb[...].astype(f32) + scale * (e - hat * jnp.mean(e * hat, axis=-1, keepdims=True))
    res[...] = dx1
    n2[...] = dx1.astype(bf16)
    dn[...] = jnp.zeros_like(dn)


    def back(step):
        slot = (units_f + step) % SLOTS[0]
        cos, sin = cos_ref[...], sin_ref[...]
        s = (z + 1 + step) % mp
        out_rows(s)
        place("B", step, 0)
        dc = nt(n2[...], outs[...])
        dc = [jnp.where(lower, t, 0.0).astype(bf16) for t in (dc[:, 0:128], swap(dc[:, 0:128]), dc[:, 128:256])]
        of_out = nn(ctx[s, 0 : heads * HEAD, :], n2[...]).astype(bf16)
        for h in range(heads):
            gbuf[slot, tall * h + 3 * HEAD : tall * h + 4 * HEAD, :] = of_out[HEAD * h : HEAD * h + HEAD]
        for h in range(heads):
            place("B", step, 1 + 2 * h)
            qh, dch = q[s, h], dc[h]
            dk_sum[...] = jnp.zeros_like(dk_sum)
            dv_sum[...] = jnp.zeros_like(dv_sum)
            for a, b in blocks:
                scores = nt(k[s, h, 0:b, :], qh[a:b]) + mask[0:b, a:b]
                p = jnp.exp(scores - lse[s, h : h + 1, a:b])
                dprob = nt(v[s, h, 0:b, :], dch[a:b])
                delta = jnp.sum(p * dprob, axis=0, keepdims=True)
                ds = (p * (dprob - delta)).astype(bf16)
                dv_sum[0:b, :] += nn(p.astype(bf16), dch[a:b])
                dk_sum[0:b, :] += nn(ds, qh[a:b])
                heads_t[0:HEAD, a:b] = nn(kt[s, h, :, 0:b], ds)
            d = heads_t[...].T * 0.125 + swap(dk_sum[...])
            made[:, 0:128] = (d * cos - turned(d, low) * sin).astype(bf16)
            made[:, 128:256] = dv_sum[...].astype(bf16)
            turned_rows[0:256, :] = made[:, 0:256].T
            place("B", step, 2 + 2 * h)
            gbuf[slot, tall * h : tall * h + 3 * HEAD, :] = nn(turned_rows[0 : 3 * HEAD, :], n1[...]).astype(bf16)
            place("B", step, 7 + h)
            dn[...] += nn(made[:, 0:256], w[0, s, tall * h : tall * h + tall, :])

    run_steps("B", back)


    place("E", 0, 0)
    x = padded(x_ref).astype(f32)
    scale = scale_of(x)
    hat = x * scale
    d1 = dn[...]
    gain_in[0, 0:1, :] = jnp.sum(d1 * hat, axis=0, keepdims=True)
    place("E", 0, 1)
    e = d1 * gain(g1_ref)
    dx = res[...] + scale * (e - hat * jnp.mean(e * hat, axis=-1, keepdims=True))
    staged[:, 0, :] = dx[0:seq]
    out_dx = pltpu.make_async_copy(staged, dx_ref, out_sem.at[0])
    out_dx.start()
    place("E", 0, 2)
    for j in range(mp):
        acc[...] += nn(hb[j], w[2, pick(table, z, j), 0:512, :])
        place("E", 0, 3 + j)
    out_dx.wait()
    staged[:, 0, :] = acc[0:seq, :]
    out_y = pltpu.make_async_copy(staged, out_ref, out_sem.at[1])
    out_y.start()
    place("E", 0, 3 + mp)
    gather_drain()
    home_drain()
    for which in range(1, 3 + heads):
        finish_drain(which)
    out_y.wait()


def rotary(rows):
    position = np.arange(rows).astype(np.float32)
    index = np.arange(HEAD // 2).astype(np.float32)
    freq = (np.float32(10000.0) ** (np.float32(-2.0) * index / np.float32(HEAD))).astype(np.float32)
    angle = position[:, None] * freq[None, :]
    angle = np.concatenate([angle] * 4, axis=-1)
    return np.cos(angle).astype(np.float32), np.sin(angle).astype(np.float32)


def layer(mp, lengths, tokens, cotangent, gain1, gain2, weights):
    _, seq, width = tokens.shape
    T = (seq + 15) // 16 * 16
    cosine, sine = rotary(T)
    vmem, anywhere = pl.BlockSpec(memory_space=pltpu.VMEM), pl.BlockSpec(memory_space=pl.ANY)
    V, DMA = pltpu.VMEM, pltpu.SemaphoreType.DMA
    half, quarter, eighth = width // 2, width // 4, width // 8
    heads = weights[0].shape[0] // HEAD
    scratch = [
        V((3, mp, width, width), bf16),
        V((T, width), bf16),
        V((T, width), bf16),
        V((width, T), bf16),
        V((T, width), bf16),
        V((mp, heads, T, 128), bf16),
        V((mp, heads, T, 128), bf16),
        V((mp, heads, T, 128), bf16),
        V((mp, heads, HEAD, T), bf16),
        V((mp, 256, T), bf16),
        V((256, width), bf16),
        V((128, T), f32),
        V((mp, 8, T), f32),
        V((T, T), f32),
        V((mp, T, 512), bf16),
        V((512, T), bf16),
        V((T, 1024), bf16),
        V((T, width), f32),
        V((T, width), f32),
        V((T, width), f32),
        V((T, 128), f32),
        V((T, 128), f32),
        V((SLOTS[0], width, width), bf16),
        V((SLOTS[1], half, width), bf16),
        V((SLOTS[2], quarter, width), bf16),
        V((SLOTS[3], eighth, width), bf16),
        V((3, mp, eighth, width), bf16),
        V((3, eighth, width), bf16),
        V((3 + mp, 8, width), f32),
        V((seq, 1, width), f32),
        DMA((4 * heads + 6,)),
        DMA((mp, heads)),
        DMA((mp, heads)),
        DMA((mp, heads, 3)),
        DMA((mp, heads, 3)),
        DMA((3, mp)),
        DMA((3, mp)),
        DMA((3, mp, 3)),
        DMA((3, mp, 3)),
        DMA((2 * mp + heads * mp, 3)),
        DMA((2 * mp + heads * mp, 3)),
        DMA((2 * mp + heads * mp,)),
        DMA((3 + heads, mp)),
        DMA((3 + heads,)),
        DMA((3 + heads, 3)),
        DMA((3 + heads, 3)),
        DMA((2 + mp,)),
        DMA((2 + mp,)),
        DMA((2,)),
        pltpu.SemaphoreType.REGULAR((3,)),
    ]
    return pl.pallas_call(
        functools.partial(kernel, mp, T),
        out_shape=(
            jax.ShapeDtypeStruct((seq, 1, width), f32),
            jax.ShapeDtypeStruct((seq, 1, width), f32),
            jax.ShapeDtypeStruct((width,), f32),
            jax.ShapeDtypeStruct((width,), f32),
            jax.ShapeDtypeStruct((3, width, width), bf16),
        ),
        in_specs=[pl.BlockSpec(memory_space=pltpu.SMEM)] + [vmem] * 6 + [anywhere] * 7,
        out_specs=[anywhere, anywhere, vmem, vmem, anywhere],
        scratch_shapes=scratch,
        compiler_params=pltpu.CompilerParams(
            collective_id=0, has_side_effects=True, vmem_limit_bytes=63 * 2**20
        ),
    )(lengths, tokens, cotangent, gain1, gain2, jnp.asarray(cosine), jnp.asarray(sine), *weights)


def tidy_kernel(
    cols, hidden, out_in, dx_in, ga_in, gm_in, fin, out, dx, ga, gm, gq, gk, gv, go, gg, gu, gd, a, b, c, big, row, sems
):
    seq, width = out.shape[0], out.shape[2]
    first = width - hidden
    rest = hidden - first
    come = [pltpu.make_async_copy(src, row.at[i], sems.at[i]) for i, src in enumerate((out_in, dx_in))]
    go_on = [pltpu.make_async_copy(row.at[i], dst, sems.at[2 + i]) for i, dst in enumerate((out, dx))]
    loads = [pltpu.make_async_copy(fin.at[i], t, sems.at[4 + i]) for i, t in enumerate((a, b, c))]
    for copy in (*loads, *come):
        copy.start()
    ga[...] = ga_in[...]
    gm[...] = gm_in[...]
    stores = []

    def store(src, dst):
        copy = pltpu.make_async_copy(src, dst, sems.at[7 + len(stores)])
        copy.start()
        stores.append(copy)

    loads[0].wait()
    heads = cols // HEAD
    for i, dst in enumerate((gq, gk, gv, go)):
        for h in range(heads):
            at_row, from_row = i * cols + h * HEAD, h * (width // heads) + i * HEAD
            big[0, at_row : at_row + HEAD, :] = a[from_row : from_row + HEAD, :].astype(f32)
        store(big.at[0, pl.ds(i * cols, cols)], dst)
    loads[1].wait()
    big[1, :, 0:hidden] = b[:, 0:hidden].astype(f32)
    store(big.at[1, :, pl.ds(0, hidden)], gg)
    loads[2].wait()
    big[2, 0:hidden, :] = c[0:hidden, :].astype(f32)
    store(big.at[2, pl.ds(0, hidden)], gd)
    for first_half, second_half in zip(come, go_on):
        first_half.wait()
        second_half.start()
    big[3, :, 0:first] = b[:, hidden:].astype(f32)
    tall = width - hidden
    for j in range(width // rest):
        big[3, j * tall : j * tall + tall, first:hidden] = c[hidden:, j * rest : j * rest + rest].astype(f32)
    store(big.at[3, :, pl.ds(0, hidden)], gu)
    for copy in (*go_on, *stores):
        copy.wait()


def tidy(cols, hidden, out, dx, ga, gm, fin):
    seq, _, width = out.shape
    vmem, anywhere = pl.BlockSpec(memory_space=pltpu.VMEM), pl.BlockSpec(memory_space=pl.ANY)
    shapes = [(seq, 1, width)] * 2 + [(width,)] * 2 + [(cols, width)] * 4 + [(width, hidden)] * 2 + [(hidden, width)]
    return pl.pallas_call(
        functools.partial(tidy_kernel, cols, hidden),
        out_shape=tuple(jax.ShapeDtypeStruct(shape, f32) for shape in shapes),
        in_specs=[anywhere, anywhere, vmem, vmem, anywhere],
        out_specs=[anywhere, anywhere, vmem, vmem] + [anywhere] * 7,
        scratch_shapes=[pltpu.VMEM((width, width), fin.dtype)] * 3
        + [
            pltpu.VMEM((4, width, width), f32),
            pltpu.VMEM((2, seq, 1, width), f32),
            pltpu.SemaphoreType.DMA((14,)),
        ],
        compiler_params=pltpu.CompilerParams(vmem_limit_bytes=60 * 2**20),
    )(out, dx, ga, gm, fin)


def per_device(mp, dp, tokens, lengths, gain1, gain2, wq, wk, wv, wo, wg, wu, wd, cotangent):
    _, seq, width = tokens.shape
    weights = (wq.T, wk.T, wv.T, wo, wg, wu, wd)
    out, dx, gain_a, gain_m, fin = layer(mp, lengths, tokens, cotangent, gain1, gain2, weights)
    if dp > 8:
        groups = [[8 * i + j for i in range(dp // 8)] for j in range(8)]
        fin, gain_a, gain_m = lax.psum((fin.astype(f32), gain_a, gain_m), "dp", axis_index_groups=groups)
    cols, hidden = wq.shape[1], wg.shape[1]
    out, dx, gain_a, gain_m, gq, gk, gv, go, gg, gu, gd = tidy(cols, hidden, out, dx, gain_a, gain_m, fin)
    items = (1, seq, width)
    return out.reshape(items), dx.reshape(items), gain_a, gain_m, gq.T, gk.T, gv.T, go, gg, gu, gd


def solution(mesh):
    rows, cols, items = P("mp", None), P(None, "mp"), P(("dp", "mp"), None, None)
    return jax.shard_map(
        functools.partial(per_device, mesh.shape["mp"], mesh.shape["dp"]),
        mesh=mesh,
        in_specs=(items, P("dp"), P(), P(), cols, cols, cols, rows, cols, cols, rows, items),
        out_specs=(items, items, P(), P(), cols, cols, cols, rows, cols, cols, rows),
        check_vma=False,
    )
```

profile of v0, /device:TPU:0, one launch (start us, length us, event | category | flops | bytes accessed | tf_op | source)
XLA Modules:
  0.0 168.0 jit_solution(12684113439467805289)
XLA Ops:
  0.6 159.0 %shard_map.221 = (f32[577,1,768]{2,1,0:T(1,128)}, f32[577,1,768]{2,1,0:T(1,128)}, f32[768]{0:T(1024)}, f32[768]{0:T(1024)}, bf16[3,768,768]{2,1,0:T(8,128)(2,1)}) custom-call(s32[4]{0:T(128)} %len_ref.1, bf16[1,577,768]{2,1,0:T(8,128)(2,1)} %x_ref.1, bf16[1,577,768]{2,1,0:T(8,128)(2,1)} %dy_ref.1, f32[768]{0:T(1024)} %g1_ref.1, f32[768]{0:T(1024)} %g2_ref.1, ...), custom_call_target="tpu_custom_call" | custom-call | tf_op jit(solution)/shard_map/pallas_call | solution.py:760
  159.7 8.1 %shard_map.222 = (f32[577,1,768]{2,1,0:T(1,128)}, f32[577,1,768]{2,1,0:T(1,128)}, f32[768]{0:T(1024)}, f32[768]{0:T(1024)}, f32[192,768]{1,0:T(8,128)}, /*index=...) custom-call(f32[577,1,768]{2,1,0:T(1,128)} %get-tuple-element.27.out, ...), custom_call_target="tpu_custom_call" | custom-call | tf_op jit(solution)/shard_map/pallas_call | solution.py:827
where the time goes:
time: 170 us; the launch traced here: 168 us
  Pallas kernels  167 us (98%)
    pallas_call x1, Pallas kernels, layer(): pl.pallas_call(functools.partial(kernel, mp, T), out_shape=(jax.ShapeDtyp...  159 us
    pallas_call x1, Pallas kernels, tidy(): pl.pallas_call(functools.partial(tidy_kernel, cols, hidden), out_shape=tu...  8.12 us

commit v1 on v0

--- a/solution.py
+++ b/solution.py
@@ -15,57 +15,58 @@
 f32, bf16 = jnp.float32, jnp.bfloat16
 LOOPED = ("A", "F", "B")
 SLOTS = (3, 6, 8, 12)
-STEPS = ((3, 3, 3), (2, 3, 3), (2, 3, 3))
+STEPS = ((3, 3, 3), (2, 3, 3), (3, 3, 2))
 
 PLAN = {
     ("P", 0, 0): (("s", 0),),
-    ("A", 0, 0): (("s", 1),),
-    ("A", 0, 2): (("a", 1, 0, 0),),
-    ("A", 1, 0): (("a", 1, 1, 0), ("a", 1, 2, 0), ("a", 1, 0, 1), ("a", 2, 0, 0), ("a", 2, 1, 0), ("a", 1, 1, 1), ("a", 1, 2, 1), ("a", 2, 0, 1), ("a", 2, 2, 0), ("a", 1, 0, 2), ("a", 1, 0, 3), ("a", 3, 0, 0),),
-    ("A", 1, 1): (("a", 2, 1, 1), ("a", 3, 1, 0), ("a", 1, 1, 2), ("a", 1, 2, 2), ("a", 2, 2, 1), ("a", 2, 0, 2), ("a", 1, 1, 3), ("a", 3, 0, 1), ("a", 1, 2, 3), ("a", 3, 2, 0),),
-    ("A", 1, 2): (("a", 2, 0, 3), ("s", 2),),
-    ("A", 2, 0): (("a", 2, 1, 2), ("a", 3, 1, 1),),
-    ("A", 2, 1): (("a", 2, 1, 3), ("a", 2, 2, 2), ("a", 3, 0, 2), ("a", 3, 2, 1), ("g", 1, 1, 0),),
-    ("A", 2, 2): (("a", 2, 2, 3), ("a", 3, 0, 3),),
-    ("A", 3, 0): (("a", 3, 1, 2), ("g", 1, 2, 0),),
-    ("A", 3, 1): (("a", 3, 1, 3), ("a", 3, 2, 2),),
-    ("A", 3, 2): (("a", 3, 2, 3), ("g", 1, 1, 1), ("g", 1, 3, 0),),
-    ("F", 0, 0): (("g", 1, 1, 2), ("g", 1, 2, 1),),
-    ("F", 0, 2): (("p", 0), ("g", 1, 3, 1), ("g", 2, 1, 0),),
-    ("F", 0, 3): (("g", 2, 2, 0),),
-    ("F", 0, 4): (("p", 1), ("t", 0, 0),),
-    ("F", 1, 0): (("g", 1, 2, 2), ("t", 1, 0), ("g", 2, 3, 0), ("g", 1, 2, 3), ("g", 2, 2, 1), ("g", 1, 3, 2), ("g", 2, 3, 1), ("g", 2, 1, 1), ("g", 1, 3, 3), ("g", 2, 1, 2),),
-    ("F", 1, 2): (("p", 2), ("t", 0, 1), ("t", 1, 1),),
-    ("F", 1, 3): (("g", 2, 2, 2),),
-    ("F", 1, 4): (("p", 3), ("g", 2, 3, 2), ("t", 2, 0),),
-    ("F", 2, 0): (("g", 2, 2, 3),),
-    ("F", 2, 1): (("g", 2, 3, 3), ("t", 3, 0), ("t", 0, 2), ("t", 1, 2),),
-    ("F", 2, 2): (("p", 4),),
-    ("F", 2, 4): (("p", 5), ("t", 2, 1), ("t", 4, 0),),
-    ("F", 3, 1): (("t", 3, 1), ("t", 5, 0),),
+    ("A", 0, 1): (("s", 1),),
+    ("A", 0, 2): (("a", 1, 0, 0), ("a", 1, 1, 0),),
+    ("A", 0, 3): (("a", 1, 2, 0),),
+    ("A", 1, 0): (("a", 1, 0, 1), ("a", 1, 1, 1), ("a", 2, 0, 0), ("a", 1, 2, 1), ("a", 2, 1, 0), ("a", 2, 2, 0), ("a", 2, 0, 1), ("a", 1, 0, 2), ("a", 3, 0, 0), ("a", 1, 1, 2), ("a", 1, 0, 3), ("a", 2, 1, 1), ("a", 1, 2, 2), ("a", 1, 1, 3), ("a", 3, 1, 0), ("a", 2, 2, 1), ("a", 1, 2, 3),),
+    ("A", 1, 1): (("a", 2, 0, 2), ("a", 3, 0, 1), ("a", 3, 2, 0), ("a", 2, 1, 2),),
+    ("A", 1, 2): (("a", 2, 0, 3), ("a", 2, 1, 3), ("a", 2, 2, 2), ("a", 3, 1, 1),),
+    ("A", 1, 3): (("a", 2, 2, 3), ("a", 3, 2, 1), ("a", 3, 0, 2), ("g", 1, 1, 0),),
+    ("A", 2, 0): (("a", 3, 0, 3), ("a", 3, 1, 2), ("s", 2),),
+    ("A", 2, 1): (("a", 3, 1, 3), ("g", 1, 2, 0), ("a", 3, 2, 2),),
+    ("A", 2, 2): (("a", 3, 2, 3),),
+    ("A", 2, 3): (("g", 1, 1, 1), ("g", 1, 3, 0), ("g", 1, 2, 1),),
+    ("A", 3, 0): (("g", 2, 1, 0), ("g", 1, 1, 2),),
+    ("A", 3, 3): (("g", 1, 3, 1),),
+    ("F", 0, 0): (("g", 2, 1, 1), ("g", 2, 2, 0), ("g", 1, 2, 2),),
+    ("F", 0, 1): (("g", 1, 2, 3),),
+    ("F", 0, 2): (("p", 0),),
+    ("F", 0, 3): (("g", 1, 3, 2), ("t", 0, 0), ("g", 2, 2, 1), ("g", 1, 3, 3), ("g", 2, 1, 2),),
+    ("F", 0, 4): (("p", 1), ("g", 2, 1, 3), ("g", 2, 3, 0),),
+    ("F", 1, 0): (("t", 1, 0),),
+    ("F", 1, 2): (("p", 2),),
+    ("F", 1, 3): (("t", 0, 1), ("t", 2, 0), ("g", 2, 2, 2),),
+    ("F", 1, 4): (("p", 3), ("g", 2, 2, 3),),
+    ("F", 2, 0): (("t", 3, 0),),
+    ("F", 2, 1): (("g", 2, 3, 1), ("t", 1, 1), ("t", 0, 2),),
+    ("F", 2, 2): (("p", 4), ("g", 2, 3, 2),),
+    ("F", 2, 4): (("p", 5), ("t", 4, 0), ("t", 2, 1),),
+    ("F", 3, 0): (("t", 5, 0), ("t", 1, 2), ("t", 3, 1),),
     ("F", 3, 2): (("p", 6),),
     ("F", 3, 4): (("p", 7), ("t", 2, 2), ("t", 6, 0),),
-    ("B", 0, 0): (("t", 7, 0),),
-    ("B", 0, 7): (("p", 8), ("t", 3, 2), ("t", 4, 1),),
-    ("B", 0, 8): (("p", 9), ("t", 5, 1), ("t", 8, 0),),
-    ("B", 0, 9): (("p", 10), ("t", 6, 1), ("t", 9, 0),),
-    ("B", 1, 7): (("p", 11), ("t", 4, 2), ("t", 5, 2), ("t", 7, 1), ("t", 8, 1), ("t", 10, 0), ("t", 11, 0), ("t", 9, 1), ("t", 6, 2),),
-    ("B", 1, 8): (("p", 12),),
-    ("B", 1, 9): (("p", 13), ("t", 8, 2), ("t", 9, 2), ("t", 12, 0), ("t", 10, 1), ("t", 11, 1), ("t", 7, 2), ("t", 13, 0),),
-    ("B", 2, 7): (("p", 14),),
-    ("B", 2, 8): (("p", 15), ("t", 10, 2), ("t", 11, 2), ("t", 12, 1), ("t", 13, 1), ("t", 14, 0),),
-    ("B", 2, 9): (("p", 16), ("t", 15, 0),),
-    ("B", 3, 7): (("p", 17), ("t", 12, 2), ("t", 13, 2), ("t", 14, 1), ("t", 15, 1), ("t", 16, 0), ("f", 1, 0), ("t", 17, 0),),
-    ("B", 3, 8): (("p", 18),),
-    ("B", 3, 9): (("p", 19), ("t", 14, 2), ("t", 15, 2), ("t", 18, 0),),
-    ("E", 0, 0): (("t", 16, 1), ("t", 17, 1), ("t", 19, 0), ("f", 1, 1), ("f", 2, 0),),
-    ("E", 0, 1): (("n", 0),),
-    ("E", 0, 2): (("n", 1),),
-    ("E", 0, 3): (("t", 18, 1), ("t", 16, 2),),
-    ("E", 0, 4): (("t", 17, 2),),
-    ("E", 0, 5): (("n", 2), ("t", 19, 1),),
-    ("E", 0, 6): (("f", 3, 0),),
-    ("E", 0, 7): (("t", 18, 2), ("f", 2, 1), ("f", 4, 0), ("n", 3), ("f", 1, 2), ("t", 19, 2), ("f", 5, 0), ("f", 3, 1), ("f", 1, 3), ("f", 4, 1), ("n", 4), ("f", 5, 1), ("f", 3, 2), ("f", 2, 2), ("f", 3, 3), ("f", 4, 2), ("f", 5, 2), ("f", 2, 3), ("f", 4, 3), ("f", 5, 3),),
+    ("M", 0, 0): (("t", 7, 0), ("t", 3, 2), ("t", 4, 1),),
+    ("B", 0, 0): (("t", 5, 1),),
+    ("B", 0, 8): (("t", 6, 1), ("t", 4, 2),),
+    ("B", 0, 9): (("p", 8), ("t", 5, 2), ("t", 7, 1), ("t", 6, 2), ("t", 8, 0),),
+    ("B", 1, 7): (("t", 7, 2),),
+    ("B", 1, 8): (("t", 8, 1),),
+    ("B", 1, 9): (("p", 9),),
+    ("B", 2, 7): (("t", 8, 2), ("t", 9, 0),),
+    ("B", 2, 9): (("p", 10), ("f", 1, 0),),
+    ("B", 3, 0): (("t", 9, 1), ("t", 10, 0),),
+    ("B", 3, 7): (("p", 11), ("f", 1, 1), ("f", 2, 0), ("t", 9, 2), ("t", 11, 0),),
+    ("B", 3, 8): (("p", 12), ("t", 10, 1),),
+    ("B", 3, 9): (("p", 13), ("t", 12, 0), ("f", 2, 1), ("t", 11, 1), ("t", 13, 0),),
+    ("E", 0, 0): (("f", 1, 2), ("t", 10, 2),),
+    ("E", 0, 1): (("n", 0), ("f", 1, 3), ("t", 11, 2), ("n", 1), ("t", 12, 1),),
+    ("E", 0, 2): (("t", 13, 1), ("f", 2, 2), ("n", 2), ("t", 12, 2), ("f", 3, 0), ("f", 4, 0), ("f", 2, 3), ("t", 13, 2), ("f", 5, 0), ("n", 3),),
+    ("E", 0, 3): (("f", 3, 1), ("f", 4, 1),),
+    ("E", 0, 4): (("f", 5, 1), ("n", 4),),
+    ("E", 0, 7): (("f", 3, 2), ("f", 4, 2), ("f", 5, 2), ("f", 3, 3), ("f", 4, 3), ("f", 5, 3),),
 }
 
 
@@ -175,7 +176,7 @@
     credit,
 ):
     seq, width = x_ref.shape[1], x_ref.shape[2]
-    half, quarter, eighth = width // 2, width // 4, width // 8
+    half, quarter = width // 2, width // 4
     heads = wq_ref.shape[0] // HEAD
     tall = width // heads
     blocks = [(a, min(a + 256, T)) for a in range(0, T, 256)]
@@ -275,14 +276,16 @@
                     across(kind, j, shard, stage).wait_send()
 
 
+    whole = units - 1
+
     def unit_of(u):
-        return u if u < units_f else units_f + (u - units_f) // heads
-
-    def head_of(u):
-        return (u - units_f) % heads
+        return min(u, whole)
+
+    def block_of(u):
+        return pl.ds(0, heads) if u < whole else pl.ds(u - whole, 1)
 
     def shard_of(u):
-        return pick(table, z, u // 2) if u < units_f else (z + 1 + (u - units_f) // heads) % mp
+        return pick(table, z, u // 2) if u < units_f else (z + 1 + u - units_f) % mp
 
     def kind_of(u):
         return 1 + u % 2 if u < units_f else 0
@@ -292,17 +295,12 @@
     given = (1 - core, 1 - far_bit, 1 - near_bit)
     kept = (core, far_bit, near_bit)
 
-    def size_of(u, stage):
-        whole = width if u < units_f else tall
-        h = 0 if u < units_f else head_of(u)
-        return whole >> (stage + 1), h * (whole >> stage), h * (whole >> (stage + 1))
-
     def give(u, stage):
-        size, before, after = size_of(u, stage)
-        unit = unit_of(u)
+        size = tall >> (stage + 1)
+        unit, block = unit_of(u), block_of(u)
         return remote(
-            stores[stage].at[unit % SLOTS[stage], at(before + given[stage] * size, size)],
-            stores[stage + 1].at[unit % SLOTS[stage + 1], at(after, size)],
+            stores[stage].at[unit % SLOTS[stage], block, at(given[stage] * size, size)],
+            stores[stage + 1].at[unit % SLOTS[stage + 1], block],
             s_send.at[u, stage],
             s_recv.at[u, stage],
             hops_back[stage],
@@ -310,12 +308,12 @@
         )
 
     def start_give(u, stage):
-        if unit_of(u) >= SLOTS[stage + 1] and (u < units_f or head_of(u) == 0):
+        if unit_of(u) >= SLOTS[stage + 1] and u <= whole:
             pl.semaphore_wait(credit.at[stage], 1)
         give(u, stage).start()
 
     def release(u, stage):
-        if unit_of(u) + SLOTS[stage + 1] < units and (u < units_f or head_of(u) == heads - 1):
+        if unit_of(u) + SLOTS[stage + 1] < units:
             pl.semaphore_signal(
                 credit.at[stage], inc=1, device_id={"dp": hops_back[stage], "mp": z}, device_id_type=MESH
             )
@@ -325,80 +323,71 @@
         copy.wait_recv()
         copy.wait_send()
         mine, came = stores[stage], stores[stage + 1]
-        unit = unit_of(u)
-        here, there = unit % SLOTS[stage], unit % SLOTS[stage + 1]
-        size, before, after = size_of(u, stage)
-        step = size >> (2 - stage)
-
-        def add(i, carry):
-            to = at(after + i * step, step)
-            sums = mine[here, at(before + kept[stage] * size + i * step, step), :].astype(f32)
-            came[there, to, :] = (sums + came[there, to, :].astype(f32)).astype(bf16)
+        here, there = unit_of(u) % SLOTS[stage], unit_of(u) % SLOTS[stage + 1]
+        size = tall >> (stage + 1)
+
+        def add(block, carry):
+            sums = mine[here, block, at(kept[stage] * size, size), :].astype(f32) + came[there, block].astype(f32)
+            came[there, block] = sums.astype(bf16)
             return carry
 
-        lax.fori_loop(0, (4, 2, 1)[stage], add, 0)
+        if u < whole:
+            lax.fori_loop(0, heads, add, 0)
+        else:
+            add(u - whole, 0)
         if stage > 0:
             release(u, stage - 1)
         if stage < 2:
             start_give(u, stage + 1)
         elif own_shard(u):
-            rows = pl.ds(after, size)
-            r4[kind_of(u), z, rows, :] = r3[there, rows, :]
+            r4[kind_of(u), z, block_of(u)] = r3[there, block_of(u)]
         else:
             home(u).start()
 
     def own_shard(u):
-        return u < 2 or u >= units_f + (mp - 1) * heads
+        return u < 2 or u >= whole
 
     def home(u):
-        size, _, after = size_of(u, 2)
-        kind, rows = kind_of(u), pl.ds(after, size)
-        arrived = kind if u < units_f else 3 + head_of(u)
-        return remote(
-            r3.at[unit_of(u) % SLOTS[3], rows],
-            r4.at[kind, z, rows],
-            h_send.at[u],
-            h_recv.at[arrived, z],
-            dp_at,
-            shard_of(u),
+        kind = kind_of(u)
+        return remote(r3.at[u % SLOTS[3]], r4.at[kind, z], h_send.at[u], h_recv.at[kind, z], dp_at, shard_of(u))
+
+    def home_drain():
+        for u in range(2, whole):
+            home(u).wait_send()
+
+
+    def sum_block(which):
+        return (which, pl.ds(0, heads)) if which < 3 else (0, pl.ds(which - 3, 1))
+
+    tall_spans = spans(0, tall)
+
+    def fin_own(which):
+        kind, block = sum_block(which)
+        return pltpu.make_async_copy(
+            total.at[kind, block], fin_ref.at[kind, block, tall_spans[0][1]], fin_sem.at[which]
         )
 
-    def home_drain():
-        for u in range(units_f + mp * heads):
-            if not own_shard(u):
-                home(u).wait_send()
-
-
-    def sum_rows(which):
-        if which < 3:
-            return which, pl.ds(0, eighth), widening
-        return 0, pl.ds((which - 3) * (tall // 8), tall // 8), by_head[which - 3]
-
-    def fin_own(which):
-        kind, rows, spans_of = sum_rows(which)
-        return pltpu.make_async_copy(total.at[kind, rows], fin_ref.at[kind, spans_of[0][1]], fin_sem.at[which])
-
     def fin_across(which, stage):
-        kind, own_rows, spans_of = sum_rows(which)
-        to, rows = spans_of[stage]
-        src = total.at[kind, own_rows] if stage == 0 else fin_ref.at[kind, rows]
-        return remote(src, fin_ref.at[kind, rows], f_send.at[which, stage], f_recv.at[which, stage], to, z)
+        kind, block = sum_block(which)
+        to, rows = tall_spans[stage]
+        dst = fin_ref.at[kind, block, rows]
+        src = total.at[kind, block] if stage == 0 else dst
+        return remote(src, dst, f_send.at[which, stage], f_recv.at[which, stage], to, z)
 
     def finish(which, stage):
-        kind, rows, _ = sum_rows(which)
+        kind, block = sum_block(which)
         if stage == 0:
-            for src in range(mp):
-
-                @pl.when(z != src)
-                def _(src=src):
-                    remote(
-                        r3.at[0, rows], r4.at[kind, src, rows], h_send.at[0], h_recv.at[which, src], dp_at, src
-                    ).wait_recv()
-
-            sums = r4[kind, 0, rows, :].astype(f32)
+            if which <= 3:
+                for src in range(mp):
+
+                    @pl.when(z != src)
+                    def _(src=src):
+                        remote(r3.at[0], r4.at[kind, src], h_send.at[0], h_recv.at[kind, src], dp_at, src).wait_recv()
+
+            sums = r4[kind, 0, block].astype(f32)
             for src in range(1, mp):
-                sums = sums + r4[kind, src, rows, :].astype(f32)
-            total[kind, rows, :] = sums.astype(bf16)
+                sums = sums + r4[kind, src, block].astype(f32)
+            total[kind, block] = sums.astype(bf16)
             fin_own(which).start()
         else:
             if stage == 1:
@@ -593,15 +582,15 @@
             made[:, part] = (dhid * up * sigma * (1.0 + gate * (1.0 - sigma))).astype(bf16)
             made[:, 512 + 256 * i : 768 + 256 * i] = (dhid * active).astype(bf16)
         place("F", step, 1)
-        gbuf[u0 % SLOTS[0]] = nn(n2t[...], made[:, 0:768]).astype(bf16)
+        gbuf[u0 % SLOTS[0]] = nn(n2t[...], made[:, 0:768]).astype(bf16).reshape(heads, tall, width)
         place("F", step, 2)
         turned_rows[0:512, :] = hb[step].T
         dn[...] += nt(made[:, 0:768], w1[...])
         place("F", step, 3)
-        gbuf[u1 % SLOTS[0], 0:512, :] = nn(turned_rows[0:512, :], dyb[...]).astype(bf16)
+        gbuf[u1 % SLOTS[0], 0:2] = nn(turned_rows[0:512, :], dyb[...]).astype(bf16).reshape(2, tall, width)
         for j in range(3):
             part = slice(256 * j, 256 * j + 256)
-            gbuf[u1 % SLOTS[0], 512:768, part] = nn(n2t[part, :], made[:, 768:1024]).astype(bf16)
+            gbuf[u1 % SLOTS[0], 2, :, part] = nn(n2t[part, :], made[:, 768:1024]).astype(bf16)
         place("F", step, 4)
         for j in range(3):
             part = slice(256 * j, 256 * j + 256)
@@ -633,7 +622,7 @@
         dc = [jnp.where(lower, t, 0.0).astype(bf16) for t in (dc[:, 0:128], swap(dc[:, 0:128]), dc[:, 128:256])]
         of_out = nn(ctx[s, 0 : heads * HEAD, :], n2[...]).astype(bf16)
         for h in range(heads):
-            gbuf[slot, tall * h + 3 * HEAD : tall * h + 4 * HEAD, :] = of_out[HEAD * h : HEAD * h + HEAD]
+            gbuf[slot, h, 3 * HEAD : 4 * HEAD, :] = of_out[HEAD * h : HEAD * h + HEAD]
         for h in range(heads):
             place("B", step, 1 + 2 * h)
             qh, dch = q[s, h], dc[h]
@@ -653,7 +642,7 @@
             made[:, 128:256] = dv_sum[...].astype(bf16)
             turned_rows[0:256, :] = made[:, 0:256].T
             place("B", step, 2 + 2 * h)
-            gbuf[slot, tall * h : tall * h + 3 * HEAD, :] = nn(turned_rows[0 : 3 * HEAD, :], n1[...]).astype(bf16)
+            gbuf[slot, h, 0 : 3 * HEAD, :] = nn(turned_rows[0 : 3 * HEAD, :], n1[...]).astype(bf16)
             place("B", step, 7 + h)
             dn[...] += nn(made[:, 0:256], w[0, s, tall * h : tall * h + tall, :])
 
@@ -703,8 +692,8 @@
     cosine, sine = rotary(T)
     vmem, anywhere = pl.BlockSpec(memory_space=pltpu.VMEM), pl.BlockSpec(memory_space=pl.ANY)
     V, DMA = pltpu.VMEM, pltpu.SemaphoreType.DMA
-    half, quarter, eighth = width // 2, width // 4, width // 8
     heads = weights[0].shape[0] // HEAD
+    tall = width // heads
     scratch = [
         V((3, mp, width, width), bf16),
         V((T, width), bf16),
@@ -728,12 +717,12 @@
         V((T, width), f32),
         V((T, 128), f32),
         V((T, 128), f32),
-        V((SLOTS[0], width, width), bf16),
-        V((SLOTS[1], half, width), bf16),
-        V((SLOTS[2], quarter, width), bf16),
-        V((SLOTS[3], eighth, width), bf16),
-        V((3, mp, eighth, width), bf16),
-        V((3, eighth, width), bf16),
+        V((SLOTS[0], heads, tall, width), bf16),
+        V((SLOTS[1], heads, tall // 2, width), bf16),
+        V((SLOTS[2], heads, tall // 4, width), bf16),
+        V((SLOTS[3], heads, tall // 8, width), bf16),
+        V((3, mp, heads, tall // 8, width), bf16),
+        V((3, heads, tall // 8, width), bf16),
         V((3 + mp, 8, width), f32),
         V((seq, 1, width), f32),
         DMA((4 * heads + 6,)),
@@ -745,10 +734,10 @@
         DMA((3, mp)),
         DMA((3, mp, 3)),
         DMA((3, mp, 3)),
-        DMA((2 * mp + heads * mp, 3)),
-        DMA((2 * mp + heads * mp, 3)),
-        DMA((2 * mp + heads * mp,)),
-        DMA((3 + heads, mp)),
+        DMA((3 * mp - 1 + heads, 3)),
+        DMA((3 * mp - 1 + heads, 3)),
+        DMA((3 * mp - 1,)),
+        DMA((3, mp)),
         DMA((3 + heads,)),
         DMA((3 + heads, 3)),
         DMA((3 + heads, 3)),
@@ -764,7 +753,7 @@
             jax.ShapeDtypeStruct((seq, 1, width), f32),
             jax.ShapeDtypeStruct((width,), f32),
             jax.ShapeDtypeStruct((width,), f32),
-            jax.ShapeDtypeStruct((3, width, width), bf16),
+            jax.ShapeDtypeStruct((3, heads, tall, width), bf16),
         ),
         in_specs=[pl.BlockSpec(memory_space=pltpu.SMEM)] + [vmem] * 6 + [anywhere] * 7,
         out_specs=[anywhere, anywhere, vmem, vmem, anywhere],
@@ -847,6 +836,7 @@
         groups = [[8 * i + j for i in range(dp // 8)] for j in range(8)]
         fin, gain_a, gain_m = lax.psum((fin.astype(f32), gain_a, gain_m), "dp", axis_index_groups=groups)
     cols, hidden = wq.shape[1], wg.shape[1]
+    fin = fin.reshape(3, width, width)
     out, dx, gain_a, gain_m, gq, gk, gv, go, gg, gu, gd = tidy(cols, hidden, out, dx, gain_a, gain_m, fin)
     items = (1, seq, width)
     return out.reshape(items), dx.reshape(items), gain_a, gain_m, gq.T, gk.T, gv.T, go, gg, gu, gd

time: 170 us -> 167 us (0.982)
  Pallas kernels: 167 us -> 164 us
    pallas_call x1, Pallas kernels: 159 us -> 156 us  [layer(): pl.pallas_call(functools.partial(kernel, mp, T), out_shape=(jax.ShapeDtyp...]
where the time goes in v1:
time: 167 us; the launch traced here: 165 us
  Pallas kernels  164 us (98%)
    pallas_call x1, Pallas kernels, layer(): pl.pallas_call(functools.partial(kernel, mp, T), out_shape=(jax.ShapeDtyp...  156 us
    pallas_call x1, Pallas kernels, tidy(): pl.pallas_call(functools.partial(tidy_kernel, cols, hidden), out_shape=tu...  8.12 us

profile of v1, /device:TPU:0, one launch (start us, length us, event | category | flops | bytes accessed | tf_op | source)
XLA Modules:
  0.0 165.0 jit_solution(9195427884095541559)
XLA Ops:
  0.6 156.0 %shard_map.221 = (f32[577,1,768]{2,1,0:T(1,128)}, f32[577,1,768]{2,1,0:T(1,128)}, f32[768]{0:T(1024)}, f32[768]{0:T(1024)}, bf16[3,3,256,768]{3,2,1,0:T(8,128)(2,1)}) custom-call(s32[4]{0:T(128)} %len_ref.1, bf16[1,577,768]{2,1,0:T(8,128)(2,1)} %x_ref.1, bf16[1,577,768]{2,1,0:T(8,128)(2,1)} %dy_ref.1, f32[768]{0:T(1024)} %g1_ref.1, f32[768]{0:T(1024)} %g2_ref.1, ...), custom_call_target="tpu_custom_call" | custom-call | tf_op jit(solution)/shard_map/pallas_call | solution.py:749
  156.7 8.1 %shard_map.222 = (f32[577,1,768]{2,1,0:T(1,128)}, f32[577,1,768]{2,1,0:T(1,128)}, f32[768]{0:T(1024)}, f32[768]{0:T(1024)}, f32[192,768]{1,0:T(8,128)}, /*index=...) custom-call(f32[577,1,768]{2,1,0:T(1,128)} %get-tuple-element.27.out, ...), custom_call_target="tpu_custom_call" | custom-call | tf_op jit(solution)/shard_map/pallas_call | solution.py:816

commit v2 on v1

--- a/solution.py
+++ b/solution.py
@@ -773,7 +773,7 @@
     come = [pltpu.make_async_copy(src, row.at[i], sems.at[i]) for i, src in enumerate((out_in, dx_in))]
     go_on = [pltpu.make_async_copy(row.at[i], dst, sems.at[2 + i]) for i, dst in enumerate((out, dx))]
     loads = [pltpu.make_async_copy(fin.at[i], t, sems.at[4 + i]) for i, t in enumerate((a, b, c))]
-    for copy in (*loads, *come):
+    for copy in (loads[0], *come, *loads[1:]):
         copy.start()
     ga[...] = ga_in[...]
     gm[...] = gm_in[...]
@@ -791,15 +791,15 @@
             at_row, from_row = i * cols + h * HEAD, h * (width // heads) + i * HEAD
             big[0, at_row : at_row + HEAD, :] = a[from_row : from_row + HEAD, :].astype(f32)
         store(big.at[0, pl.ds(i * cols, cols)], dst)
+    for first_half, second_half in zip(come, go_on):
+        first_half.wait()
+        second_half.start()
     loads[1].wait()
     big[1, :, 0:hidden] = b[:, 0:hidden].astype(f32)
     store(big.at[1, :, pl.ds(0, hidden)], gg)
     loads[2].wait()
     big[2, 0:hidden, :] = c[0:hidden, :].astype(f32)
     store(big.at[2, pl.ds(0, hidden)], gd)
-    for first_half, second_half in zip(come, go_on):
-        first_half.wait()
-        second_half.start()
     big[3, :, 0:first] = b[:, hidden:].astype(f32)
     tall = width - hidden
     for j in range(width // rest):

time: 167 us -> 167 us (level)
  no operation moved by 1% of the time
where the time goes in v2:
time: 167 us; the launch traced here: 165 us
  Pallas kernels  164 us (98%)
    pallas_call x1, Pallas kernels, layer(): pl.pallas_call(functools.partial(kernel, mp, T), out_shape=(jax.ShapeDtyp...  156 us
    pallas_call x1, Pallas kernels, tidy(): pl.pallas_call(functools.partial(tidy_kernel, cols, hidden), out_shape=tu...  8.14 us

profile of v2, /device:TPU:0, one launch (start us, length us, event | category | flops | bytes accessed | tf_op | source)
XLA Modules:
  0.0 165.0 jit_solution(8197300884720996960)
XLA Ops:
  0.6 156.0 %shard_map.221 = (f32[577,1,768]{2,1,0:T(1,128)}, f32[577,1,768]{2,1,0:T(1,128)}, f32[768]{0:T(1024)}, f32[768]{0:T(1024)}, bf16[3,3,256,768]{3,2,1,0:T(8,128)(2,1)}) custom-call(s32[4]{0:T(128)} %len_ref.1, bf16[1,577,768]{2,1,0:T(8,128)(2,1)} %x_ref.1, bf16[1,577,768]{2,1,0:T(8,128)(2,1)} %dy_ref.1, f32[768]{0:T(1024)} %g1_ref.1, f32[768]{0:T(1024)} %g2_ref.1, ...), custom_call_target="tpu_custom_call" | custom-call | tf_op jit(solution)/shard_map/pallas_call | solution.py:749
  156.7 8.1 %shard_map.222 = (f32[577,1,768]{2,1,0:T(1,128)}, f32[577,1,768]{2,1,0:T(1,128)}, f32[768]{0:T(1024)}, f32[768]{0:T(1024)}, f32[192,768]{1,0:T(8,128)}, /*index=...) custom-call(f32[577,1,768]{2,1,0:T(1,128)} %get-tuple-element.27.out, ...), custom_call_target="tpu_custom_call" | custom-call | tf_op jit(solution)/shard_map/pallas_call | solution.py:816
